TPU v7x, 512 devices: a whole 4x8x8 slice. The times are simulated.
512 devices in a mesh: ctx: 16 (over z, core), kvh: 8 (over y), tp: 4 (over x).
Axes of the slice: x: 4, y: 8, z: 8, core: 2. Of those that a mesh axis runs over, the one named last changes fastest.
Arguments:
- prefill_cache: bfloat16 [2, 32, 8192, 1024], P(None, None, ('ctx', 'tp'), 'kvh'), may hold values from -4 to 4
- lengths: int32 [32], replicated, may hold values from 1 to 8192, 163840 in all
- slot_of: int32 [32], replicated, may hold values from 0 to 31, each once
- queries: bfloat16 [4, 32, 16384], P(None, 'ctx', ('kvh', 'tp')), may hold values from -100 to 100
- new_kv: bfloat16 [2, 4, 32, 1024], P(None, None, 'ctx', 'kvh'), may hold values from -4 to 4
Outputs:
- attended: bfloat16 [4, 32, 16384], P(None, 'ctx', ('kvh', 'tp'))
- decode_cache: bfloat16 [2, 32, 8192, 1024], P(None, 'ctx', 'tp', 'kvh')
Inputs may be any that keep to these rules, and one draw needn't show every extreme that they name: `lengths`: each request has at least one live position; the longest request fills all 8192 slots. `slot_of`: each slot is given to exactly one request.
All inputs are finite; a program needn't handle non-finite values.
Results may differ from a plain program's by a relative error of at most 0.011.
Values may be sent and summed in bfloat16 or wider, within the bound.
A program may use at most 64 MiB of HBM per device.

v0:
```python
import math

import jax
import jax.numpy as jnp
from jax import lax
from jax.sharding import PartitionSpec as P

HD = 128
STEPS = 4


def block_terms(query_rows, key_rows, value_rows, valid):
    scores = jnp.einsum(
        "srkgd,rpkd->rkgsp", query_rows, key_rows, preferred_element_type=jnp.float32
    )
    scores = jnp.where(valid, scores * (1.0 / math.sqrt(HD)), -1e30)
    top = jnp.max(scores, axis=-1)
    weights = jnp.where(valid, jnp.exp(scores - top[..., None]), 0.0)
    total = jnp.sum(weights, axis=-1)
    summed = jnp.einsum(
        "rkgsp,rpkd->rkgsd",
        weights.astype(jnp.bfloat16),
        value_rows,
        preferred_element_type=jnp.float32,
    )
    return (top, total, summed)


def combine_parts(first, second):
    top = jnp.maximum(first[0], second[0])
    first_scale = jnp.exp(first[0] - top)
    second_scale = jnp.exp(second[0] - top)
    total = first[1] * first_scale + second[1] * second_scale
    summed = first[2] * first_scale[..., None] + second[2] * second_scale[..., None]
    return (top, total, summed)


def shards(prefill_cache, lengths, slot_of, queries, new_kv):
    count = slot_of.shape[0]
    order = jnp.arange(count, dtype=jnp.int32)
    matches = slot_of[None, :] == order[:, None]
    inverse = jnp.sum(jnp.where(matches, order[None, :], 0), axis=1)
    slot_lengths = jnp.sum(jnp.where(matches, lengths[None, :], 0), axis=1)
    local_reqs = queries.shape[1]
    mine = lax.dynamic_slice_in_dim(slot_lengths, lax.axis_index("ctx") * local_reqs, local_reqs)
    block = prefill_cache.shape[2]
    kv_here = prefill_cache.shape[3] // HD
    tp_count = lax.axis_size("tp")
    steps_idx = jnp.arange(STEPS, dtype=jnp.int32)
    causal = (steps_idx[None, :] <= steps_idx[:, None])[None, None, None]
    ordered = jnp.take(prefill_cache, inverse, axis=1)
    received = lax.all_to_all(ordered, "ctx", split_axis=1, concat_axis=2, tiled=True)
    stride = received.shape[2]
    fresh_keys = new_kv[0].reshape(STEPS, local_reqs, kv_here, HD).transpose(1, 0, 2, 3)
    fresh_values = new_kv[1].reshape(STEPS, local_reqs, kv_here, HD).transpose(1, 0, 2, 3)
    gathered = lax.all_gather(received, "tp", axis=2, tiled=True)
    span = gathered.shape[2]
    key_rows = gathered[0].reshape(local_reqs, span, kv_here, HD)
    value_rows = gathered[1].reshape(local_reqs, span, kv_here, HD)
    own_heads = queries.shape[2] // HD
    query_rows = queries.reshape(STEPS, local_reqs, 1, own_heads, HD)
    places = jnp.arange(span, dtype=jnp.int32)
    global_places = (
        places % stride // block * tp_count + places // stride
    ) * block + places % block
    valid = (global_places[None, :] < mine[:, None])[:, None, None, None, :]
    cached = block_terms(query_rows, key_rows, value_rows, valid)
    recent = block_terms(query_rows, fresh_keys, fresh_values, causal)
    top, total, summed = combine_parts(cached, recent)
    result = summed / total[..., None]
    result = jnp.transpose(result, (3, 0, 1, 2, 4)).reshape(STEPS, local_reqs, own_heads * HD)
    attended = result.astype(jnp.bfloat16)
    return (attended, received)


def solution(mesh):
    return jax.shard_map(
        shards,
        mesh=mesh,
        in_specs=(
            P(None, None, ("ctx", "tp"), "kvh"),
            P(),
            P(),
            P(None, "ctx", ("kvh", "tp")),
            P(None, None, "ctx", "kvh"),
        ),
        out_specs=(P(None, "ctx", ("kvh", "tp")), P(None, "ctx", "tp", "kvh")),
        check_vma=False,
    )
```

profile of v0, /device:TPU:1, one launch (start us, length us, event | category | flops | bytes accessed | tf_op | source)
XLA Modules:
  0.0 177.5 jit_solution(14480390337345585701)
XLA Ops:
  7.2 0.0 copy-start
  7.2 0.0 all-gather.2.cloned.1.call-start
  7.2 0.9 select_reduce_fusion.1
  8.2 0.6 copy-done
  8.8 2.1 %gather_fusion = bf16[32,2,128,128]{3,2,1,0:T(8,128)(2,1)} fusion(bf16[2,32,128,128]{3,2,1,0:T(8,128)(2,1)S(1)} %copy-done, s32[1024]{0:T(1024)S(1)} %pad_clamp_fusion), kind=kCustom, calls=%fused_computation | custom fusion | bytes 4194432 | tf_op jit(solution)/shard_map/jit(_take)/gather | solution.py:51
  10.9 1.8 %select_bitcast_fusion = bf16[2,32,128,128]{3,2,0,1:T(8,128)(2,1)S(1)} fusion(bf16[32,2,128,128]{3,2,1,0:T(8,128)(2,1)} %gather_fusion, pred[32]{0:T(512)(128)(4,1)S(1)} %compare_and_fusion), kind=kLoop, calls=%fused_computation.8 | loop fusion | flops 1048576 | bytes 4194336 | tf_op jit(solution)/shard_map/jit(_take)/select_n | solution.py:51
  12.8 62.7 %all_to_all.18 = bf16[2,32,128,128]{3,2,0,1:T(8,128)(2,1)S(1)} all-to-all(bf16[2,32,128,128]{3,2,0,1:T(8,128)(2,1)S(1)} %select_bitcast_fusion), channel_id=1, replica_groups=mesh['ctx'=16,'kvh'=8,'tp'=4] {'ctx'}, dimensions={1} | all-to-all | bytes 4194304 | tf_op jit(solution)/shard_map/all_to_all | solution.py:52
  75.4 1.5 copy.30
  76.9 0.0 copy-start.1
  76.9 0.0 copy-start.2
  76.9 0.0 all-gather.2.cloned.1.call-update
  76.9 0.7 copy-done.1
  77.6 0.1 dynamic_slice.3
  77.7 0.0 copy-done.2
  77.7 0.2 convolution_multiply_fusion.2
  77.9 0.1 fusion.37
  78.0 0.1 convert_bitcast_fusion
  78.1 0.1 broadcast_compare_fusion
  78.2 83.8 %all-gather.2.cloned.1.call-done = bf16[2,2,8192,128]{3,2,1,0:T(8,128)(2,1)} async-done(((bf16[2,2,2048,128]{3,2,1,0:T(8,128)(2,1)}), bf16[2,2,8192,128]{3,2,1,0:T(8,128)(2,1)}) %all-gather.2.cloned.1.call-update) | async-done | bytes 8388624 | tf_op jit(solution)/shard_map/all_gather | solution.py:56
  162.0 3.7 %fusion.49 = (f32[2,4,4]{1,2,0:T(4,128)S(1)}, f32[2,1,4,4,8192]{4,2,3,0,1:T(4,128)S(1)}) fusion(bf16[4,2,4,128]{3,2,1,0:T(4,128)(2,1)S(1)} %reshape.216, bf16[2,2,8192,128]{3,2,1,0:T(8,128)(2,1)} %all-gather.2.cloned.1.call-done, pred[2,8192]{1,0:T(4,128)(4,1)S(1)} %broadcast_compare_fusion), kind=kOutput, calls=%fused_computation.80 | convolution fusion | flops 67895264 | bytes 5267584 | tf_op jit(solution)/shard_map/srkgd,rpkd->rkgsp/dot_general | solution.py:13
  165.8 0.7 fusion.9
  166.5 3.3 %fusion.6 = f32[2,4,4,128]{3,1,2,0:T(4,128)S(1)} fusion(bf16[2,2,8192,128]{3,2,1,0:T(8,128)(2,1)} %all-gather.2.cloned.1.call-done, f32[2,1,4,4,8192]{4,2,3,0,1:T(4,128)S(1)} %get-tuple-element.12, f32[2,4,4]{1,2,0:T(4,128)S(1)} %get-tuple-element.11, pred[2,8192]{1,0:T(4,128)(4,1)S(1)} %broadcast_compare_fusion, f32[2,4,4]{1,2,0:T(4,128)S(1)} %bitcast.95), kind=kOutput, calls=%fused_computation.13 | convolution fusion | flops 67899392 | bytes 5275904 | tf_op jit(solution)/shard_map/rkgsp,rpkd->rkgsd/dot_general | solution.py:20
  169.8 0.2 fusion.8
  170.0 0.6 copy.47
  (9 shorter events, 0.1 us)
Async XLA Ops:
  7.2 1.6 copy-start
  7.2 154.9 %all-gather.2.cloned.1.call-start = ((), (), s32[]{:S(2)}) async-start(), calls=%async_computation.1 | async-start | bytes 10485760 | tf_op jit(solution)/shard_map/all_gather | solution.py:56
  76.9 0.7 copy-start.1
  76.9 0.8 copy-start.2
Sparse Core Ops, SparseCore 0:
  77.0 84.9 all-gather.1
where the time goes:
time: 178 us; the launch traced here: 177 us
  waiting for transfers between devices  83.8 us (47%)
  blocking collectives  62.7 us (35%)
  between operations  14.1 us (8%)
  matrix products  7.42 us (4%)
  local copies, waits for them, and re-layouts  5.6 us (3%)
  other arithmetic  3.83 us (2%)
    all_gather x1, waiting for transfers between devices, shards(): gathered = lax.all_gather(received, 'tp', axis=2, tiled=True)  83.8 us
    all_to_all x1, blocking collectives, shards(): lax.all_to_all(ordered, 'ctx', split_axis=1, concat_axis=2, tiled=True)  62.7 us
    dot_general x2, matrix products, block_terms(): jnp.einsum('srkgd,rpkd->rkgsp', query_rows, key_rows, preferred_element_t...  3.91 us
  transfers between devices with their start and end apart: 1, of which 1 were waited for; matrix products, arithmetic and copies ran while one was open for 0% of the time, Pallas kernels for 0%

commit v1 on v0

v1 whole, which is shorter than its diff:
```python
import math

import jax
import jax.numpy as jnp
from jax import lax
from jax.experimental import pallas as pl
from jax.experimental.pallas import tpu as pltpu
from jax.sharding import PartitionSpec as P

HD = 128
STEPS = 4
SCALE = 1.0 / math.sqrt(HD)
MESH = pl.DeviceIdType.MESH
DEAD = -1e38
FLOOR = -1e30


def kernel(
    cache_ref, slot_ref, len_ref, query_ref, new_ref,
    out_ref, rec_ref,
    raw, stage, own_q, all_q, mail, running, box,
    load_sem, send_sem, recv_sem, q_send_sem, q_recv_sem, mail_send_sem, mail_recv_sem,
):
    me = lax.axis_index("ctx")
    tp = lax.axis_index("tp")
    z, core = me // 2, lax.rem(me, 2)
    n_ctx = lax.axis_size("ctx")
    n_tp = lax.axis_size("tp")
    chips = n_ctx // 2
    requests = slot_ref.shape[0]
    slots = requests // n_ctx
    block = cache_ref.shape[2]
    own_heads = query_ref.shape[2] // HD
    rows = STEPS * own_heads

    load = pltpu.make_async_copy(cache_ref, raw, load_sem)
    load.start()

    def partner(dz, other):
        return lax.rem(z + dz, chips) * 2 + (1 - core if other else core)

    barrier = pltpu.get_barrier_semaphore()
    for k in range(1, n_ctx):
        pl.semaphore_signal(
            barrier, inc=1, device_id={"ctx": lax.rem(me + k, n_ctx)}, device_id_type=MESH
        )
    for k in range(1, n_tp):
        pl.semaphore_signal(
            barrier, inc=1, device_id={"tp": lax.rem(tp + k, n_tp)}, device_id_type=MESH
        )

    for j in range(slots):
        for s in range(STEPS):
            for h in range(own_heads):
                own_q[j, s * own_heads + h, :] = query_ref[
                    s, j, h * HD : (h + 1) * HD
                ].astype(jnp.float32)
    all_q[:, pl.ds(tp * rows, rows), :] = own_q[...].astype(jnp.bfloat16)

    def request_of(slot):
        found = jnp.int32(0)
        for r in range(1, requests):
            found = jnp.where(slot_ref[r] == slot, r, found)
        return found

    def fill(d):
        for j in range(slots):
            r = request_of(d * slots + j)
            for k in range(2):
                stage[d, k, j] = raw[k, r]

    def to(d):
        return pltpu.make_async_remote_copy(
            src_ref=stage.at[d],
            dst_ref=rec_ref.at[:, :, pl.ds(me * block, block)],
            send_sem=send_sem.at[d],
            recv_sem=recv_sem.at[me],
            device_id={"ctx": d},
            device_id_type=MESH,
        )

    def arrived(d):
        pltpu.make_async_remote_copy(
            src_ref=stage.at[d],
            dst_ref=rec_ref.at[:, :, pl.ds(d * block, block)],
            send_sem=send_sem.at[d],
            recv_sem=recv_sem.at[d],
            device_id={"ctx": d},
            device_id_type=MESH,
        ).wait_recv()

    def q_copy(owner, t):
        here = all_q.at[:, pl.ds(owner * rows, rows)]
        return pltpu.make_async_remote_copy(
            src_ref=here, dst_ref=here,
            send_sem=q_send_sem.at[t], recv_sem=q_recv_sem.at[owner],
            device_id={"tp": t}, device_id_type=MESH,
        )

    def mail_copy(owner, t):
        return pltpu.make_async_remote_copy(
            src_ref=mail.at[:, :, pl.ds(t * rows, rows)], dst_ref=box.at[owner],
            send_sem=mail_send_sem.at[t], recv_sem=mail_recv_sem.at[owner],
            device_id={"tp": t}, device_id_type=MESH,
        )

    load.wait()
    first = partner(0, True)
    fill(first)
    pl.semaphore_wait(barrier, n_ctx - 1 + n_tp - 1)

    to(first).start()
    for k in range(1, n_tp):
        q_copy(tp, lax.rem(tp + k, n_tp)).start()

    def send_round(k, carry):
        for other in (False, True):
            for dz in (k, chips - k):
                d = partner(dz, other)
                fill(d)
                to(d).start()
        return carry

    lax.fori_loop(1, chips // 2, send_round, 0)
    for other in (False, True):
        d = partner(chips // 2, other)
        fill(d)
        to(d).start()

    fill(me)
    rec_ref[:, :, pl.ds(me * block, block), :] = stage[me]

    row_step = lax.broadcasted_iota(jnp.int32, (rows, HD), 0) // own_heads
    for j in range(slots):
        queries = own_q[j]
        scores = []
        for u in range(STEPS):
            key = new_ref[0, u, j, :].astype(jnp.float32).reshape(1, HD)
            dots = jnp.sum(queries * key, axis=1, keepdims=True)
            scores.append(jnp.where(row_step >= u, jnp.broadcast_to(dots, (rows, HD)), DEAD))
        top = scores[0]
        for u in range(1, STEPS):
            top = jnp.maximum(top, scores[u])
        total = jnp.zeros((rows, HD), jnp.float32)
        summed = jnp.zeros((rows, HD), jnp.float32)
        for u in range(STEPS):
            weight = jnp.exp((scores[u] - top) * SCALE)
            value = new_ref[1, u, j, :].astype(jnp.float32).reshape(1, HD)
            total = total + weight
            summed = summed + weight.astype(jnp.bfloat16).astype(jnp.float32) * value
        box[n_tp, 0, j] = summed
        box[n_tp, 1, j] = top
        running[2, j, 0:rows] = total

    lengths = [len_ref[request_of(me * slots + j)] for j in range(slots)]
    mail[0] = jnp.zeros(mail.shape[1:], jnp.float32)
    running[0] = jnp.full(running.shape[1:], FLOOR, jnp.float32)
    running[1] = jnp.zeros(running.shape[1:], jnp.float32)

    for k in range(1, n_tp):
        t = lax.rem(tp + k, n_tp)
        q_copy(t, t).wait_recv()

    span = 2 * block
    lane = lax.broadcasted_iota(jnp.int32, (n_tp * rows, span), 1)
    place = (lane // block) * (n_tp * block) + lax.rem(lane, block)

    def attend(chip):
        at = pl.ds(pl.multiple_of(chip * span, span), span)
        base = (chip * 2 * n_tp + tp) * block
        for j in range(slots):
            scores = lax.dot_general(
                all_q[j], rec_ref[0, j, at, :], (((1,), (1,)), ((), ())),
                preferred_element_type=jnp.float32,
            )
            scores = jnp.where(place < lengths[j] - base, scores, DEAD)
            before = running[0, j]
            top = jnp.maximum(before, jnp.max(scores, axis=1, keepdims=True))
            weights = jnp.exp((scores - jnp.concatenate([top, top], axis=1)) * SCALE)
            shrink = jnp.exp((before - top) * SCALE)
            running[0, j] = top
            running[1, j] = running[1, j] * shrink + jnp.sum(weights, axis=1, keepdims=True)
            mail[0, j] = mail[0, j] * shrink + jnp.dot(
                weights.astype(jnp.bfloat16), rec_ref[1, j, at, :],
                preferred_element_type=jnp.float32,
            )

    arrived(first)
    attend(z)

    def recv_round(k, carry):
        for dz in (k, chips - k):
            arrived(partner(dz, False))
            arrived(partner(dz, True))
            attend(lax.rem(z + dz, chips))
        return carry

    lax.fori_loop(1, chips // 2, recv_round, 0)
    arrived(partner(chips // 2, False))
    arrived(partner(chips // 2, True))
    attend(lax.rem(z + chips // 2, chips))

    half = lax.broadcasted_iota(jnp.int32, mail.shape[1:], 2) < HD // 2
    mail[1] = jnp.where(half, running[0], running[1])
    for k in range(1, n_tp):
        mail_copy(tp, lax.rem(tp + k, n_tp)).start()
    box[tp] = mail[:, :, pl.ds(tp * rows, rows), :]
    for k in range(1, n_tp):
        t = lax.rem(tp + k, n_tp)
        mail_copy(t, t).wait_recv()

    for j in range(slots):
        tops, totals = [], []
        for t in range(n_tp):
            both = box[t, 1, j]
            tops.append(jnp.broadcast_to(both[:, 0:1], (rows, HD)))
            totals.append(jnp.broadcast_to(both[:, HD // 2 : HD // 2 + 1], (rows, HD)))
        tops.append(box[n_tp, 1, j])
        totals.append(running[2, j, 0:rows])
        top = tops[0]
        for other in tops[1:]:
            top = jnp.maximum(top, other)
        total = jnp.zeros((rows, HD), jnp.float32)
        summed = jnp.zeros((rows, HD), jnp.float32)
        for t in range(n_tp + 1):
            share = jnp.exp((tops[t] - top) * SCALE)
            total = total + totals[t] * share
            summed = summed + box[t, 0, j] * share
        out_ref[j] = (summed / total).astype(out_ref.dtype)

    def sent(k, carry):
        to(lax.rem(me + k, n_ctx)).wait_send()
        return carry

    lax.fori_loop(1, n_ctx, sent, 0)
    for k in range(1, n_tp):
        t = lax.rem(tp + k, n_tp)
        q_copy(tp, t).wait_send()
        mail_copy(tp, t).wait_send()


def shards(prefill_cache, lengths, slot_of, queries, new_kv):
    n_ctx, n_tp = lax.axis_size("ctx"), lax.axis_size("tp")
    _, requests, block, width = prefill_cache.shape
    slots = requests // n_ctx
    own_heads = queries.shape[2] // HD
    rows = STEPS * own_heads
    attended, received = pl.pallas_call(
        kernel,
        out_shape=(
            jax.ShapeDtypeStruct((slots, rows, HD), jnp.bfloat16),
            jax.ShapeDtypeStruct((2, slots, n_ctx * block, width), jnp.bfloat16),
        ),
        in_specs=[
            pl.BlockSpec(memory_space=pltpu.HBM),
            pl.BlockSpec(memory_space=pltpu.SMEM),
            pl.BlockSpec(memory_space=pltpu.SMEM),
            pl.BlockSpec(memory_space=pltpu.VMEM),
            pl.BlockSpec(memory_space=pltpu.VMEM),
        ],
        out_specs=(
            pl.BlockSpec(memory_space=pltpu.VMEM),
            pl.BlockSpec(memory_space=pltpu.VMEM),
        ),
        scratch_shapes=[
            pltpu.VMEM(prefill_cache.shape, jnp.bfloat16),
            pltpu.VMEM((n_ctx, 2, slots, block, width), jnp.bfloat16),
            pltpu.VMEM((slots, rows, HD), jnp.float32),
            pltpu.VMEM((slots, n_tp * rows, HD), jnp.bfloat16),
            pltpu.VMEM((2, slots, n_tp * rows, HD), jnp.float32),
            pltpu.VMEM((3, slots, n_tp * rows, HD), jnp.float32),
            pltpu.VMEM((n_tp + 1, 2, slots, rows, HD), jnp.float32),
            pltpu.SemaphoreType.DMA,
            pltpu.SemaphoreType.DMA((n_ctx,)),
            pltpu.SemaphoreType.DMA((n_ctx,)),
            pltpu.SemaphoreType.DMA((n_tp,)),
            pltpu.SemaphoreType.DMA((n_tp,)),
            pltpu.SemaphoreType.DMA((n_tp,)),
            pltpu.SemaphoreType.DMA((n_tp,)),
        ],
        compiler_params=pltpu.CompilerParams(
            collective_id=0, has_side_effects=True, vmem_limit_bytes=32 << 20
        ),
        name="handover",
    )(prefill_cache, slot_of, lengths, queries, new_kv)
    attended = attended.reshape(slots, STEPS, own_heads * HD).transpose(1, 0, 2)
    return attended, received


def solution(mesh):
    return jax.shard_map(
        shards,
        mesh=mesh,
        in_specs=(
            P(None, None, ("ctx", "tp"), "kvh"),
            P(),
            P(),
            P(None, "ctx", ("kvh", "tp")),
            P(None, None, "ctx", "kvh"),
        ),
        out_specs=(P(None, "ctx", ("kvh", "tp")), P(None, "ctx", "tp", "kvh")),
        check_vma=False,
    )
```

time: 178 us -> 71.6 us (0.40)
  waiting for transfers between devices: 83.8 us -> 0 us
  Pallas kernels: 0 us -> 63.7 us
  blocking collectives: 62.7 us -> 0 us
  between operations: 14.1 us -> 0.66 us
  matrix products: 7.42 us -> 0 us
  other arithmetic: 3.83 us -> 0 us
    all_gather x1 -> x0, waiting for transfers between devices: 83.8 us -> none  [shards(): gathered = lax.all_gather(received, 'tp', axis=2, tiled=True)]
    pallas_call x0 -> x1, Pallas kernels: none -> 63.7 us  [shards(): pl.pallas_call(kernel, out_shape=(jax.ShapeDtypeStruct((slots, rows, HD),...]
    all_to_all x1 -> x0, blocking collectives: 62.7 us -> none  [shards(): lax.all_to_all(ordered, 'ctx', split_axis=1, concat_axis=2, tiled=True)]
    dot_general x4 -> x0, matrix products: 7.42 us -> none  [the longest x2 3.91 us: block_terms(): jnp.einsum('srkgd,rpkd->rkgsp', query_rows, key_rows, preferred_element_t...]
    unnamed x6 -> x11, local copies, waits for them, and re-layouts: 1.28 us -> 5.59 us
    gather x1 -> x0, local copies, waits for them, and re-layouts: 2.13 us -> none  [shards(): ordered = jnp.take(prefill_cache, inverse, axis=1)]
    select_n x2 -> x0, other arithmetic: 1.84 us -> none  [shards(): ordered = jnp.take(prefill_cache, inverse, axis=1)]
  transfers between devices with their start and end apart: 1 -> 0, of which waited for: 1 -> 0; matrix products, arithmetic and copies ran while one was open for 0% -> 0% of each run, Pallas kernels for 0% -> 0%
where the time goes in v1:
time: 71.6 us; the launch traced here: 70.6 us
  Pallas kernels  63.7 us (89%)
  local copies, waits for them, and re-layouts  6.21 us (9%)
    pallas_call x1, Pallas kernels, shards(): pl.pallas_call(kernel, out_shape=(jax.ShapeDtypeStruct((slots, rows, HD),...  63.7 us
    unnamed x11, local copies, waits for them, and re-layouts  5.59 us

profile of v1, /device:TPU:1, one launch (start us, length us, event | category | flops | bytes accessed | tf_op | source)
XLA Modules:
  0.0 70.6 jit_solution(16995050418599901215)
XLA Ops:
  0.6 0.0 copy-start
  0.6 1.6 %copy-done = bf16[2,32,128,128]{3,2,1,0:T(8,128)(2,1)S(1)} copy-done((bf16[2,32,128,128]{3,2,1,0:T(8,128)(2,1)S(1)}, bf16[2,32,128,128]{3,2,1,0:T(8,128)(2,1)}, u32[]{:S(2)}) %copy-start) | copy-done | bytes 2097176
  2.2 0.0 copy-start.1
  2.2 0.7 copy-done.1
  2.9 0.0 copy-start.2
  2.9 0.7 copy-done.2
  3.6 0.0 copy-start.3
  3.6 0.7 copy-done.3
  4.3 0.0 copy-start.4
  4.3 0.7 copy-done.4
  4.9 63.7 %handover.1 = (bf16[2,16,128]{2,1,0:T(8,128)(2,1)S(1)}, bf16[2,2,2048,128]{3,2,1,0:T(8,128)(2,1)S(1)}) custom-call(bf16[2,32,128,128]{3,2,1,0:T(8,128)(2,1)S(1)} %copy-done, s32[32]{0:T(128)S(1)} %copy-done.3, s32[32]{0:T(128)S(1)} %copy-done.4, bf16[4,2,512]{2,1,0:T(2,128)(2,1)S(1)} %copy-done.1, bf16[2,4,2,128]{3,2,1,0:T(2,128)(2,1)S(1)} %copy-done.2), custom_call_target="tpu_custom_call" | custom-call | tf_op jit(solution)/shard_map/handover/pallas_call | solution.py:248
  68.7 0.6 copy.9
  69.3 1.3 %copy.11 = bf16[2,2,2048,128]{3,2,1,0:T(8,128)(2,1)} copy(bf16[2,2,2048,128]{3,2,1,0:T(8,128)(2,1)S(1)} %get-tuple-element.9) | data formatting | bytes 4194304
  (1 shorter events, 0.0 us)
Async XLA Ops:
  0.6 1.6 %copy-start = (bf16[2,32,128,128]{3,2,1,0:T(8,128)(2,1)S(1)}, bf16[2,32,128,128]{3,2,1,0:T(8,128)(2,1)}, u32[]{:S(2)}) copy-start(bf16[2,32,128,128]{3,2,1,0:T(8,128)(2,1)} %cache_ref.1) | copy-start | bytes 6291460
  2.2 0.7 copy-start.1
  2.9 0.7 copy-start.2
  3.6 0.7 copy-start.3
  4.3 0.7 copy-start.4

commit v2 on v1

--- a/solution.py
+++ b/solution.py
@@ -16,9 +16,9 @@
 
 
 def kernel(
-    cache_ref, slot_ref, len_ref, query_ref, new_ref,
+    cache_in, slot_in, len_in, query_in, new_in,
     out_ref, rec_ref,
-    raw, stage, own_q, all_q, mail, running, box,
+    slot_ref, len_ref, query_ref, new_ref, raw, stage, own_q, all_q, mail, running, box,
     load_sem, send_sem, recv_sem, q_send_sem, q_recv_sem, mail_send_sem, mail_recv_sem,
 ):
     me = lax.axis_index("ctx")
@@ -29,12 +29,19 @@
     chips = n_ctx // 2
     requests = slot_ref.shape[0]
     slots = requests // n_ctx
-    block = cache_ref.shape[2]
+    block = raw.shape[2]
     own_heads = query_ref.shape[2] // HD
     rows = STEPS * own_heads
 
-    load = pltpu.make_async_copy(cache_ref, raw, load_sem)
-    load.start()
+    loads = [
+        pltpu.make_async_copy(source, target, load_sem.at[i])
+        for i, (source, target) in enumerate(
+            [(slot_in, slot_ref), (cache_in, raw), (query_in, query_ref),
+             (len_in, len_ref), (new_in, new_ref)]
+        )
+    ]
+    for load in loads:
+        load.start()
 
     def partner(dz, other):
         return lax.rem(z + dz, chips) * 2 + (1 - core if other else core)
@@ -48,14 +55,6 @@
         pl.semaphore_signal(
             barrier, inc=1, device_id={"tp": lax.rem(tp + k, n_tp)}, device_id_type=MESH
         )
-
-    for j in range(slots):
-        for s in range(STEPS):
-            for h in range(own_heads):
-                own_q[j, s * own_heads + h, :] = query_ref[
-                    s, j, h * HD : (h + 1) * HD
-                ].astype(jnp.float32)
-    all_q[:, pl.ds(tp * rows, rows), :] = own_q[...].astype(jnp.bfloat16)
 
     def request_of(slot):
         found = jnp.int32(0)
@@ -104,9 +103,19 @@
             device_id={"tp": t}, device_id_type=MESH,
         )
 
-    load.wait()
+    for load in loads:
+        load.wait()
     first = partner(0, True)
     fill(first)
+
+    for j in range(slots):
+        for s in range(STEPS):
+            for h in range(own_heads):
+                own_q[j, s * own_heads + h, :] = query_ref[
+                    s, j, h * HD : (h + 1) * HD
+                ].astype(jnp.float32)
+    all_q[:, pl.ds(tp * rows, rows), :] = own_q[...].astype(jnp.bfloat16)
+
     pl.semaphore_wait(barrier, n_ctx - 1 + n_tp - 1)
 
     to(first).start()
@@ -251,18 +260,16 @@
             jax.ShapeDtypeStruct((slots, rows, HD), jnp.bfloat16),
             jax.ShapeDtypeStruct((2, slots, n_ctx * block, width), jnp.bfloat16),
         ),
-        in_specs=[
-            pl.BlockSpec(memory_space=pltpu.HBM),
-            pl.BlockSpec(memory_space=pltpu.SMEM),
-            pl.BlockSpec(memory_space=pltpu.SMEM),
-            pl.BlockSpec(memory_space=pltpu.VMEM),
-            pl.BlockSpec(memory_space=pltpu.VMEM),
-        ],
+        in_specs=[pl.BlockSpec(memory_space=pltpu.HBM)] * 5,
         out_specs=(
             pl.BlockSpec(memory_space=pltpu.VMEM),
             pl.BlockSpec(memory_space=pltpu.VMEM),
         ),
         scratch_shapes=[
+            pltpu.SMEM(slot_of.shape, jnp.int32),
+            pltpu.SMEM(lengths.shape, jnp.int32),
+            pltpu.VMEM(queries.shape, jnp.bfloat16),
+            pltpu.VMEM(new_kv.shape, jnp.bfloat16),
             pltpu.VMEM(prefill_cache.shape, jnp.bfloat16),
             pltpu.VMEM((n_ctx, 2, slots, block, width), jnp.bfloat16),
             pltpu.VMEM((slots, rows, HD), jnp.float32),
@@ -270,7 +277,7 @@
             pltpu.VMEM((2, slots, n_tp * rows, HD), jnp.float32),
             pltpu.VMEM((3, slots, n_tp * rows, HD), jnp.float32),
             pltpu.VMEM((n_tp + 1, 2, slots, rows, HD), jnp.float32),
-            pltpu.SemaphoreType.DMA,
+            pltpu.SemaphoreType.DMA((5,)),
             pltpu.SemaphoreType.DMA((n_ctx,)),
             pltpu.SemaphoreType.DMA((n_ctx,)),
             pltpu.SemaphoreType.DMA((n_tp,)),
@@ -282,7 +289,12 @@
             collective_id=0, has_side_effects=True, vmem_limit_bytes=32 << 20
         ),
         name="handover",
-    )(prefill_cache, slot_of, lengths, queries, new_kv)
+    )(
+        *(
+            pltpu.with_memory_space_constraint(array, pltpu.HBM)
+            for array in (prefill_cache, slot_of, lengths, queries, new_kv)
+        )
+    )
     attended = attended.reshape(slots, STEPS, own_heads * HD).transpose(1, 0, 2)
     return attended, received
 

time: 71.6 us -> 66.8 us (0.933)
  local copies, waits for them, and re-layouts: 6.21 us -> 1.94 us
    unnamed x11 -> x1, local copies, waits for them, and re-layouts: 5.59 us -> 1.32 us
where the time goes in v2:
time: 66.8 us; the launch traced here: 65.7 us
  Pallas kernels  63.2 us (95%)
  local copies, waits for them, and re-layouts  1.94 us (3%)
    pallas_call x1, Pallas kernels, shards(): pl.pallas_call(kernel, out_shape=(jax.ShapeDtypeStruct((slots, rows, HD),...  63.2 us

profile of v2, /device:TPU:1, one launch (start us, length us, event | category | flops | bytes accessed | tf_op | source)
XLA Modules:
  0.0 65.7 jit_solution(5191536629529358930)
XLA Ops:
  0.6 63.2 %handover.1 = (bf16[2,16,128]{2,1,0:T(8,128)(2,1)S(1)}, bf16[2,2,2048,128]{3,2,1,0:T(8,128)(2,1)S(1)}) custom-call(bf16[2,32,128,128]{3,2,1,0:T(8,128)(2,1)} %cache_in.1, s32[32]{0:T(128)} %slot_in.1, s32[32]{0:T(128)} %len_in.1, bf16[4,2,512]{2,1,0:T(2,128)(2,1)} %query_in.1, bf16[2,4,2,128]{3,2,1,0:T(2,128)(2,1)} %new_in.1), custom_call_target="tpu_custom_call" | custom-call | tf_op jit(solution)/shard_map/handover/pallas_call | solution.py:257
  63.8 0.6 copy.9
  64.4 1.3 %copy.11 = bf16[2,2,2048,128]{3,2,1,0:T(8,128)(2,1)} copy(bf16[2,2,2048,128]{3,2,1,0:T(8,128)(2,1)S(1)} %get-tuple-element.9) | data formatting | bytes 4194304
  (1 shorter events, 0.0 us)

commit v3 on v2

--- a/solution.py
+++ b/solution.py
@@ -14,12 +14,41 @@
 DEAD = -1e38
 FLOOR = -1e30
 
+SEND_ORDER = (
+    (1, 7, 4, 6, 5, 3, 2),
+    (3, 1, 7, 4, 2, 6, 5),
+    (1, 7, 4, 2, 6, 3, 5),
+    (6, 1, 7, 2, 3, 5, 4),
+    (1, 4, 5, 6, 2, 7, 3),
+    (1, 7, 4, 2, 6, 3, 5),
+    (1, 7, 5, 2, 6, 3, 4),
+    (1, 7, 4, 6, 2, 3, 5),
+)
+RECV_ORDER = (
+    (7, 4, 1, 6, 2, 3, 5),
+    (7, 2, 1, 3, 4, 6, 5),
+    (7, 1, 2, 5, 6, 3, 4),
+    (7, 3, 4, 2, 6, 1, 5),
+    (5, 1, 7, 4, 6, 2, 3),
+    (7, 1, 2, 6, 4, 3, 5),
+    (7, 1, 4, 2, 6, 5, 3),
+    (7, 1, 6, 2, 3, 5, 4),
+)
+
+
+def by_chip(orders, z, radix):
+    code = jnp.int32(0)
+    for chip, order in enumerate(orders):
+        number = sum(distance * radix**i for i, distance in enumerate(order))
+        code = code + jnp.where(z == chip, number, 0)
+    return code
+
 
 def kernel(
     cache_in, slot_in, len_in, query_in, new_in,
-    out_ref, rec_ref,
-    slot_ref, len_ref, query_ref, new_ref, raw, stage, own_q, all_q, mail, running, box,
-    load_sem, send_sem, recv_sem, q_send_sem, q_recv_sem, mail_send_sem, mail_recv_sem,
+    rec_ref, box,
+    slot_ref, len_ref, query_ref, new_ref, raw, stage, own_q, all_q, mail, running,
+    load_sem, send_sem, recv_sem, q_send_sem, q_recv_sem, mail_send_sem, mail_recv_sem, ready,
 ):
     me = lax.axis_index("ctx")
     tp = lax.axis_index("tp")
@@ -36,25 +65,31 @@
     loads = [
         pltpu.make_async_copy(source, target, load_sem.at[i])
         for i, (source, target) in enumerate(
-            [(slot_in, slot_ref), (cache_in, raw), (query_in, query_ref),
-             (len_in, len_ref), (new_in, new_ref)]
+            [(slot_in, slot_ref)]
+            + [(cache_in.at[k, pl.ds(i * 8, 8)], raw.at[k, pl.ds(i * 8, 8)]) for k in range(2) for i in range(requests // 8)]
+            + [(query_in, query_ref), (len_in, len_ref), (new_in, new_ref)]
         )
     ]
     for load in loads:
         load.start()
 
-    def partner(dz, other):
-        return lax.rem(z + dz, chips) * 2 + (1 - core if other else core)
-
     barrier = pltpu.get_barrier_semaphore()
-    for k in range(1, n_ctx):
-        pl.semaphore_signal(
-            barrier, inc=1, device_id={"ctx": lax.rem(me + k, n_ctx)}, device_id_type=MESH
-        )
     for k in range(1, n_tp):
         pl.semaphore_signal(
             barrier, inc=1, device_id={"tp": lax.rem(tp + k, n_tp)}, device_id_type=MESH
         )
+    for d in range(n_ctx):
+
+        @pl.when((d // 2 >= z) & (d != me))
+        def _():
+            pl.semaphore_signal(barrier, inc=1, device_id={"ctx": d}, device_id_type=MESH)
+
+    pl.semaphore_wait(barrier, 2 * z + 1 + n_tp - 1)
+    for d in range(n_ctx - 2):
+
+        @pl.when(d // 2 < z)
+        def _():
+            pl.semaphore_signal(ready.at[me], inc=1, device_id={"ctx": d}, device_id_type=MESH)
 
     def request_of(slot):
         found = jnp.int32(0)
@@ -105,8 +140,25 @@
 
     for load in loads:
         load.wait()
-    first = partner(0, True)
-    fill(first)
+
+    def serve(i, code):
+        chip = lax.rem(z + lax.rem(code, chips), chips)
+        for other in range(2):
+            d = chip * 2 + lax.rem(core + other, 2)
+
+            @pl.when(chip > z)
+            def _():
+                pl.semaphore_wait(ready.at[d], 1)
+
+            fill(d)
+            to(d).start()
+        return code // chips
+
+    send_code = by_chip(SEND_ORDER, z, chips)
+    twin = z * 2 + 1 - core
+    lax.fori_loop(0, chips - 1, serve, send_code)
+    fill(twin)
+    to(twin).start()
 
     for j in range(slots):
         for s in range(STEPS):
@@ -115,29 +167,15 @@
                     s, j, h * HD : (h + 1) * HD
                 ].astype(jnp.float32)
     all_q[:, pl.ds(tp * rows, rows), :] = own_q[...].astype(jnp.bfloat16)
-
-    pl.semaphore_wait(barrier, n_ctx - 1 + n_tp - 1)
-
-    to(first).start()
     for k in range(1, n_tp):
         q_copy(tp, lax.rem(tp + k, n_tp)).start()
-
-    def send_round(k, carry):
-        for other in (False, True):
-            for dz in (k, chips - k):
-                d = partner(dz, other)
-                fill(d)
-                to(d).start()
-        return carry
-
-    lax.fori_loop(1, chips // 2, send_round, 0)
-    for other in (False, True):
-        d = partner(chips // 2, other)
-        fill(d)
-        to(d).start()
 
     fill(me)
     rec_ref[:, :, pl.ds(me * block, block), :] = stage[me]
+
+    def packed(top, total):
+        lanes = lax.broadcasted_iota(jnp.int32, top.shape, len(top.shape) - 1)
+        return jnp.where(lanes < HD // 2, top, total)
 
     row_step = lax.broadcasted_iota(jnp.int32, (rows, HD), 0) // own_heads
     for j in range(slots):
@@ -158,8 +196,7 @@
             total = total + weight
             summed = summed + weight.astype(jnp.bfloat16).astype(jnp.float32) * value
         box[n_tp, 0, j] = summed
-        box[n_tp, 1, j] = top
-        running[2, j, 0:rows] = total
+        box[n_tp, 1, j] = packed(top, total)
 
     lengths = [len_ref[request_of(me * slots + j)] for j in range(slots)]
     mail[0] = jnp.zeros(mail.shape[1:], jnp.float32)
@@ -194,58 +231,74 @@
                 preferred_element_type=jnp.float32,
             )
 
-    arrived(first)
+    arrived(twin)
     attend(z)
 
-    def recv_round(k, carry):
-        for dz in (k, chips - k):
-            arrived(partner(dz, False))
-            arrived(partner(dz, True))
-            attend(lax.rem(z + dz, chips))
-        return carry
-
-    lax.fori_loop(1, chips // 2, recv_round, 0)
-    arrived(partner(chips // 2, False))
-    arrived(partner(chips // 2, True))
-    attend(lax.rem(z + chips // 2, chips))
-
-    half = lax.broadcasted_iota(jnp.int32, mail.shape[1:], 2) < HD // 2
-    mail[1] = jnp.where(half, running[0], running[1])
+    def collect(i, code):
+        chip = lax.rem(z + lax.rem(code, chips), chips)
+        arrived(chip * 2 + core)
+        arrived(chip * 2 + 1 - core)
+        attend(chip)
+        return code // chips
+
+    recv_code = by_chip(RECV_ORDER, z, chips)
+    lax.fori_loop(0, chips - 1, collect, recv_code)
+
+    mail[1] = packed(running[0], running[1])
     for k in range(1, n_tp):
         mail_copy(tp, lax.rem(tp + k, n_tp)).start()
     box[tp] = mail[:, :, pl.ds(tp * rows, rows), :]
+
+    def sent(k, carry):
+        to(lax.rem(me + k, n_ctx)).wait_send()
+        return carry
+
+    lax.fori_loop(1, n_ctx, sent, 0)
+    for k in range(1, n_tp):
+        q_copy(tp, lax.rem(tp + k, n_tp)).wait_send()
     for k in range(1, n_tp):
         t = lax.rem(tp + k, n_tp)
         mail_copy(t, t).wait_recv()
-
+        mail_copy(tp, t).wait_send()
+
+
+def finish(rec_ref, box, out_ref, cache_ref, held, sem):
+    copies = [
+        pltpu.make_async_copy(rec_ref.at[k, j], cache_ref.at[k, j], sem.at[k, j])
+        for k in range(rec_ref.shape[0])
+        for j in range(rec_ref.shape[1])
+    ]
+    for copy in copies:
+        copy.start()
+    parts, _, slots, rows, _ = box.shape
+    own_heads = rows // STEPS
+    results = []
     for j in range(slots):
         tops, totals = [], []
-        for t in range(n_tp):
+        for t in range(parts):
             both = box[t, 1, j]
             tops.append(jnp.broadcast_to(both[:, 0:1], (rows, HD)))
             totals.append(jnp.broadcast_to(both[:, HD // 2 : HD // 2 + 1], (rows, HD)))
-        tops.append(box[n_tp, 1, j])
-        totals.append(running[2, j, 0:rows])
         top = tops[0]
         for other in tops[1:]:
             top = jnp.maximum(top, other)
         total = jnp.zeros((rows, HD), jnp.float32)
         summed = jnp.zeros((rows, HD), jnp.float32)
-        for t in range(n_tp + 1):
+        for t in range(parts):
             share = jnp.exp((tops[t] - top) * SCALE)
             total = total + totals[t] * share
             summed = summed + box[t, 0, j] * share
-        out_ref[j] = (summed / total).astype(out_ref.dtype)
-
-    def sent(k, carry):
-        to(lax.rem(me + k, n_ctx)).wait_send()
-        return carry
-
-    lax.fori_loop(1, n_ctx, sent, 0)
-    for k in range(1, n_tp):
-        t = lax.rem(tp + k, n_tp)
-        q_copy(tp, t).wait_send()
-        mail_copy(tp, t).wait_send()
+        results.append(summed / total)
+    for s in range(STEPS):
+        for h in range(own_heads):
+            r = s * own_heads + h
+            piece = jnp.concatenate([result[r : r + 1] for result in results], axis=0)
+            held[s, :, h * HD : (h + 1) * HD] = piece.astype(held.dtype)
+    last = pltpu.make_async_copy(held, out_ref, sem.at[0, slots])
+    last.start()
+    last.wait()
+    for copy in copies:
+        copy.wait()
 
 
 def shards(prefill_cache, lengths, slot_of, queries, new_kv):
@@ -254,13 +307,14 @@
     slots = requests // n_ctx
     own_heads = queries.shape[2] // HD
     rows = STEPS * own_heads
-    attended, received = pl.pallas_call(
+    operands = (prefill_cache, slot_of, lengths, queries, new_kv)
+    received, box = pl.pallas_call(
         kernel,
         out_shape=(
-            jax.ShapeDtypeStruct((slots, rows, HD), jnp.bfloat16),
             jax.ShapeDtypeStruct((2, slots, n_ctx * block, width), jnp.bfloat16),
-        ),
-        in_specs=[pl.BlockSpec(memory_space=pltpu.HBM)] * 5,
+            jax.ShapeDtypeStruct((n_tp + 1, 2, slots, rows, HD), jnp.float32),
+        ),
+        in_specs=[pl.BlockSpec(memory_space=pltpu.HBM)] * len(operands),
         out_specs=(
             pl.BlockSpec(memory_space=pltpu.VMEM),
             pl.BlockSpec(memory_space=pltpu.VMEM),
@@ -275,28 +329,36 @@
             pltpu.VMEM((slots, rows, HD), jnp.float32),
             pltpu.VMEM((slots, n_tp * rows, HD), jnp.bfloat16),
             pltpu.VMEM((2, slots, n_tp * rows, HD), jnp.float32),
-            pltpu.VMEM((3, slots, n_tp * rows, HD), jnp.float32),
-            pltpu.VMEM((n_tp + 1, 2, slots, rows, HD), jnp.float32),
-            pltpu.SemaphoreType.DMA((5,)),
+            pltpu.VMEM((2, slots, n_tp * rows, HD), jnp.float32),
+            pltpu.SemaphoreType.DMA((4 + 2 * (requests // 8),)),
             pltpu.SemaphoreType.DMA((n_ctx,)),
             pltpu.SemaphoreType.DMA((n_ctx,)),
             pltpu.SemaphoreType.DMA((n_tp,)),
             pltpu.SemaphoreType.DMA((n_tp,)),
             pltpu.SemaphoreType.DMA((n_tp,)),
             pltpu.SemaphoreType.DMA((n_tp,)),
+            pltpu.SemaphoreType.REGULAR((n_ctx,)),
         ],
         compiler_params=pltpu.CompilerParams(
             collective_id=0, has_side_effects=True, vmem_limit_bytes=32 << 20
         ),
         name="handover",
-    )(
-        *(
-            pltpu.with_memory_space_constraint(array, pltpu.HBM)
-            for array in (prefill_cache, slot_of, lengths, queries, new_kv)
-        )
-    )
-    attended = attended.reshape(slots, STEPS, own_heads * HD).transpose(1, 0, 2)
-    return attended, received
+    )(*(pltpu.with_memory_space_constraint(operand, pltpu.HBM) for operand in operands))
+    return pl.pallas_call(
+        finish,
+        out_shape=(
+            jax.ShapeDtypeStruct(queries.shape, jnp.bfloat16),
+            jax.ShapeDtypeStruct(received.shape, jnp.bfloat16),
+        ),
+        in_specs=[pl.BlockSpec(memory_space=pltpu.VMEM)] * 2,
+        out_specs=(pl.BlockSpec(memory_space=pltpu.HBM), pl.BlockSpec(memory_space=pltpu.HBM)),
+        scratch_shapes=[
+            pltpu.VMEM(queries.shape, jnp.bfloat16),
+            pltpu.SemaphoreType.DMA((2, slots + 1)),
+        ],
+        compiler_params=pltpu.CompilerParams(vmem_limit_bytes=16 << 20),
+        name="finish",
+    )(received, box)
 
 
 def solution(mesh):

time: 66.8 us -> 63.8 us (0.955)
  the two profiles are of different devices: /device:TPU:1 before, /device:TPU:137 now
where the time goes in v3:
time: 63.8 us; the launch traced here: 63.7 us
  Pallas kernels  63 us (99%)
  between operations  0.64 us (1%)
    pallas_call x1, Pallas kernels, shards(): pl.pallas_call(kernel, out_shape=(jax.ShapeDtypeStruct((2, slots, n_ctx *...  61.7 us
    pallas_call x1, Pallas kernels, shards(): pl.pallas_call(finish, out_shape=(jax.ShapeDtypeStruct(queries.shape, jnp...  1.37 us

profile of v3, /device:TPU:137, one launch (start us, length us, event | category | flops | bytes accessed | tf_op | source)
XLA Modules:
  0.0 63.7 jit_solution(1891934275526246296)
XLA Ops:
  0.6 61.7 %handover.1 = (bf16[2,2,2048,128]{3,2,1,0:T(8,128)(2,1)S(1)}, f32[5,2,2,16,128]{4,3,2,1,0:T(8,128)S(1)}) custom-call(bf16[2,32,128,128]{3,2,1,0:T(8,128)(2,1)} %cache_in.1, s32[32]{0:T(128)} %slot_in.1, s32[32]{0:T(128)} %len_in.1, bf16[4,2,512]{2,1,0:T(2,128)(2,1)} %query_in.1, bf16[2,4,2,128]{3,2,1,0:T(2,128)(2,1)} %new_in.1), custom_call_target="tpu_custom_call" | custom-call | tf_op jit(solution)/shard_map/handover/pallas_call | solution.py:311
  62.3 1.4 %finish.1 = (bf16[4,2,512]{2,1,0:T(2,128)(2,1)}, bf16[2,2,2048,128]{3,2,1,0:T(8,128)(2,1)}) custom-call(bf16[2,2,2048,128]{3,2,1,0:T(8,128)(2,1)S(1)} %get-tuple-element.4.rec_ref, f32[5,2,2,16,128]{4,3,2,1,0:T(8,128)S(1)} %get-tuple-element.5.box), custom_call_target="tpu_custom_call" | custom-call | tf_op jit(solution)/shard_map/finish/pallas_call | solution.py:347

commit v4 on v3

--- a/solution.py
+++ b/solution.py
@@ -15,24 +15,25 @@
 FLOOR = -1e30
 
 SEND_ORDER = (
-    (1, 7, 4, 6, 5, 3, 2),
-    (3, 1, 7, 4, 2, 6, 5),
-    (1, 7, 4, 2, 6, 3, 5),
-    (6, 1, 7, 2, 3, 5, 4),
-    (1, 4, 5, 6, 2, 7, 3),
-    (1, 7, 4, 2, 6, 3, 5),
-    (1, 7, 5, 2, 6, 3, 4),
-    (1, 7, 4, 6, 2, 3, 5),
+    (3, 5, 2, 7, 1, 4, 6),
+    (2, 1, 4, 7, 6, 5, 3),
+    (1, 3, 7, 6, 2, 4, 5),
+    (5, 1, 2, 3, 6, 7, 4),
+    (5, 4, 2, 6, 7, 1, 3),
+    (3, 4, 7, 1, 5, 2, 6),
+    (6, 2, 5, 3, 1, 4, 7),
+    (1, 5, 4, 2, 6, 7, 3),
 )
+HOLDER, VIA, GOAL, TURN = 4, 3, 0, 4
 RECV_ORDER = (
-    (7, 4, 1, 6, 2, 3, 5),
-    (7, 2, 1, 3, 4, 6, 5),
-    (7, 1, 2, 5, 6, 3, 4),
-    (7, 3, 4, 2, 6, 1, 5),
-    (5, 1, 7, 4, 6, 2, 3),
-    (7, 1, 2, 6, 4, 3, 5),
-    (7, 1, 4, 2, 6, 5, 3),
-    (7, 1, 6, 2, 3, 5, 4),
+    (1, 5, 3, 6, 4, 7, 2),
+    (4, 3, 7, 1, 5, 2, 6),
+    (6, 2, 7, 1, 5, 3, 4),
+    (5, 7, 6, 4, 3, 2, 1),
+    (7, 1, 3, 4, 2, 5, 6),
+    (4, 6, 3, 5, 7, 2, 1),
+    (6, 7, 3, 2, 4, 1, 5),
+    (2, 1, 6, 5, 7, 3, 4),
 )
 
 
@@ -47,8 +48,8 @@
 def kernel(
     cache_in, slot_in, len_in, query_in, new_in,
     rec_ref, box,
-    slot_ref, len_ref, query_ref, new_ref, raw, stage, own_q, all_q, mail, running,
-    load_sem, send_sem, recv_sem, q_send_sem, q_recv_sem, mail_send_sem, mail_recv_sem, ready,
+    slot_ref, len_ref, query_ref, new_ref, raw, stage, passing, own_q, all_q, mail, running,
+    load_sem, send_sem, recv_sem, q_send_sem, q_recv_sem, mail_send_sem, mail_recv_sem, pass_sem, ready,
 ):
     me = lax.axis_index("ctx")
     tp = lax.axis_index("tp")
@@ -97,11 +98,10 @@
             found = jnp.where(slot_ref[r] == slot, r, found)
         return found
 
-    def fill(d):
+    def fill(d, found):
         for j in range(slots):
-            r = request_of(d * slots + j)
             for k in range(2):
-                stage[d, k, j] = raw[k, r]
+                stage[d, k, j] = raw[k, found[j]]
 
     def to(d):
         return pltpu.make_async_remote_copy(
@@ -110,6 +110,27 @@
             send_sem=send_sem.at[d],
             recv_sem=recv_sem.at[me],
             device_id={"ctx": d},
+            device_id_type=MESH,
+        )
+
+    def to_via(d):
+        return pltpu.make_async_remote_copy(
+            src_ref=stage.at[d],
+            dst_ref=passing,
+            send_sem=send_sem.at[d],
+            recv_sem=pass_sem.at[0],
+            device_id={"ctx": VIA * 2 + core},
+            device_id_type=MESH,
+        )
+
+    def pass_on():
+        source = HOLDER * 2 + core
+        return pltpu.make_async_remote_copy(
+            src_ref=passing,
+            dst_ref=rec_ref.at[:, :, pl.ds(source * block, block)],
+            send_sem=pass_sem.at[1],
+            recv_sem=recv_sem.at[source],
+            device_id={"ctx": GOAL * 2 + 1 - core},
             device_id_type=MESH,
         )
 
@@ -133,15 +154,19 @@
 
     def mail_copy(owner, t):
         return pltpu.make_async_remote_copy(
-            src_ref=mail.at[:, :, pl.ds(t * rows, rows)], dst_ref=box.at[owner],
+            src_ref=mail.at[:, pl.ds(t * rows, rows)], dst_ref=box.at[owner],
             send_sem=mail_send_sem.at[t], recv_sem=mail_recv_sem.at[owner],
             device_id={"tp": t}, device_id_type=MESH,
         )
 
-    for load in loads:
-        load.wait()
-
-    def serve(i, code):
+    def serve(i, carry):
+        code, now = carry
+
+        @pl.when((z == VIA) & (i == TURN))
+        def _():
+            to_via(GOAL * 2 + 1 - core).wait_recv()
+            pass_on().start()
+
         chip = lax.rem(z + lax.rem(code, chips), chips)
         for other in range(2):
             d = chip * 2 + lax.rem(core + other, 2)
@@ -150,15 +175,41 @@
             def _():
                 pl.semaphore_wait(ready.at[d], 1)
 
-            fill(d)
-            to(d).start()
-        return code // chips
+            fill(d, now[other * slots : (other + 1) * slots])
+            if other == 0:
+                to(d).start()
+            else:
+                around = (z == HOLDER) & (chip == GOAL)
+
+                @pl.when(around)
+                def _():
+                    to_via(d).start()
+
+                @pl.when(jnp.logical_not(around))
+                def _():
+                    to(d).start()
+
+        return code // chips, requests_of(code // chips)
+
+    def requests_of(code):
+        chip = lax.rem(z + lax.rem(code, chips), chips)
+        return tuple(
+            request_of((chip * 2 + lax.rem(core + other, 2)) * slots + j)
+            for other in range(2)
+            for j in range(slots)
+        )
 
     send_code = by_chip(SEND_ORDER, z, chips)
     twin = z * 2 + 1 - core
-    lax.fori_loop(0, chips - 1, serve, send_code)
-    fill(twin)
+    loads[0].wait()
+    first = requests_of(send_code)
+    for load in loads[1:-3]:
+        load.wait()
+    lax.fori_loop(0, chips - 1, serve, (send_code, first))
+    fill(twin, [request_of(twin * slots + j) for j in range(slots)])
     to(twin).start()
+    for load in loads[-3:]:
+        load.wait()
 
     for j in range(slots):
         for s in range(STEPS):
@@ -170,13 +221,20 @@
     for k in range(1, n_tp):
         q_copy(tp, lax.rem(tp + k, n_tp)).start()
 
-    fill(me)
-    rec_ref[:, :, pl.ds(me * block, block), :] = stage[me]
-
-    def packed(top, total):
-        lanes = lax.broadcasted_iota(jnp.int32, top.shape, len(top.shape) - 1)
-        return jnp.where(lanes < HD // 2, top, total)
-
+    own = [request_of(me * slots + j) for j in range(slots)]
+    for j in range(slots):
+        for k in range(2):
+            rec_ref[k, j, pl.ds(me * block, block), :] = raw[k, own[j]]
+
+    def packed(tops, totals):
+        bands = [both[j] for j in range(slots) for both in (tops, totals)]
+        band = lax.broadcasted_iota(jnp.int32, bands[0].shape, 1) // (HD // len(bands))
+        result = bands[0]
+        for i in range(1, len(bands)):
+            result = jnp.where(band == i, bands[i], result)
+        return result
+
+    new_tops, new_totals = [], []
     row_step = lax.broadcasted_iota(jnp.int32, (rows, HD), 0) // own_heads
     for j in range(slots):
         queries = own_q[j]
@@ -195,11 +253,13 @@
             value = new_ref[1, u, j, :].astype(jnp.float32).reshape(1, HD)
             total = total + weight
             summed = summed + weight.astype(jnp.bfloat16).astype(jnp.float32) * value
-        box[n_tp, 0, j] = summed
-        box[n_tp, 1, j] = packed(top, total)
-
-    lengths = [len_ref[request_of(me * slots + j)] for j in range(slots)]
-    mail[0] = jnp.zeros(mail.shape[1:], jnp.float32)
+        box[n_tp, j] = summed
+        new_tops.append(top)
+        new_totals.append(total)
+    box[n_tp, slots] = packed(new_tops, new_totals)
+
+    lengths = [len_ref[r] for r in own]
+    mail[...] = jnp.zeros(mail.shape, jnp.float32)
     running[0] = jnp.full(running.shape[1:], FLOOR, jnp.float32)
     running[1] = jnp.zeros(running.shape[1:], jnp.float32)
 
@@ -214,22 +274,36 @@
     def attend(chip):
         at = pl.ds(pl.multiple_of(chip * span, span), span)
         base = (chip * 2 * n_tp + tp) * block
-        for j in range(slots):
-            scores = lax.dot_general(
+        each = range(slots)
+        scores = [
+            lax.dot_general(
                 all_q[j], rec_ref[0, j, at, :], (((1,), (1,)), ((), ())),
                 preferred_element_type=jnp.float32,
             )
-            scores = jnp.where(place < lengths[j] - base, scores, DEAD)
-            before = running[0, j]
-            top = jnp.maximum(before, jnp.max(scores, axis=1, keepdims=True))
-            weights = jnp.exp((scores - jnp.concatenate([top, top], axis=1)) * SCALE)
-            shrink = jnp.exp((before - top) * SCALE)
-            running[0, j] = top
-            running[1, j] = running[1, j] * shrink + jnp.sum(weights, axis=1, keepdims=True)
-            mail[0, j] = mail[0, j] * shrink + jnp.dot(
-                weights.astype(jnp.bfloat16), rec_ref[1, j, at, :],
+            for j in each
+        ]
+        scores = [jnp.where(place < lengths[j] - base, scores[j], DEAD) for j in each]
+        before = [running[0, j] for j in each]
+        top = [jnp.maximum(before[j], jnp.max(scores[j], axis=1, keepdims=True)) for j in each]
+        weights = [
+            jnp.exp((scores[j] - jnp.concatenate([top[j], top[j]], axis=1)) * SCALE) for j in each
+        ]
+        summed = [
+            jnp.dot(
+                weights[j].astype(jnp.bfloat16), rec_ref[1, j, at, :],
                 preferred_element_type=jnp.float32,
             )
+            for j in each
+        ]
+        shrink = [jnp.exp((before[j] - top[j]) * SCALE) for j in each]
+        totals = [
+            running[1, j] * shrink[j] + jnp.sum(weights[j], axis=1, keepdims=True) for j in each
+        ]
+        summed = [mail[j] * shrink[j] + summed[j] for j in each]
+        for j in each:
+            running[0, j] = top[j]
+            running[1, j] = totals[j]
+            mail[j] = summed[j]
 
     arrived(twin)
     attend(z)
@@ -244,16 +318,21 @@
     recv_code = by_chip(RECV_ORDER, z, chips)
     lax.fori_loop(0, chips - 1, collect, recv_code)
 
-    mail[1] = packed(running[0], running[1])
+    mail[slots] = packed([running[0, j] for j in range(slots)], [running[1, j] for j in range(slots)])
     for k in range(1, n_tp):
         mail_copy(tp, lax.rem(tp + k, n_tp)).start()
-    box[tp] = mail[:, :, pl.ds(tp * rows, rows), :]
+    box[tp] = mail[:, pl.ds(tp * rows, rows), :]
 
     def sent(k, carry):
         to(lax.rem(me + k, n_ctx)).wait_send()
         return carry
 
     lax.fori_loop(1, n_ctx, sent, 0)
+
+    @pl.when(z == VIA)
+    def _():
+        pass_on().wait_send()
+
     for k in range(1, n_tp):
         q_copy(tp, lax.rem(tp + k, n_tp)).wait_send()
     for k in range(1, n_tp):
@@ -270,15 +349,18 @@
     ]
     for copy in copies:
         copy.start()
-    parts, _, slots, rows, _ = box.shape
+    parts, rows = box.shape[0], box.shape[2]
+    slots = box.shape[1] - 1
+    band = HD // (2 * slots)
     own_heads = rows // STEPS
     results = []
     for j in range(slots):
         tops, totals = [], []
         for t in range(parts):
-            both = box[t, 1, j]
-            tops.append(jnp.broadcast_to(both[:, 0:1], (rows, HD)))
-            totals.append(jnp.broadcast_to(both[:, HD // 2 : HD // 2 + 1], (rows, HD)))
+            bands = box[t, slots]
+            at = 2 * j * band
+            tops.append(jnp.broadcast_to(bands[:, at : at + 1], (rows, HD)))
+            totals.append(jnp.broadcast_to(bands[:, at + band : at + band + 1], (rows, HD)))
         top = tops[0]
         for other in tops[1:]:
             top = jnp.maximum(top, other)
@@ -287,7 +369,7 @@
         for t in range(parts):
             share = jnp.exp((tops[t] - top) * SCALE)
             total = total + totals[t] * share
-            summed = summed + box[t, 0, j] * share
+            summed = summed + box[t, j] * share
         results.append(summed / total)
     for s in range(STEPS):
         for h in range(own_heads):
@@ -312,7 +394,7 @@
         kernel,
         out_shape=(
             jax.ShapeDtypeStruct((2, slots, n_ctx * block, width), jnp.bfloat16),
-            jax.ShapeDtypeStruct((n_tp + 1, 2, slots, rows, HD), jnp.float32),
+            jax.ShapeDtypeStruct((n_tp + 1, slots + 1, rows, HD), jnp.float32),
         ),
         in_specs=[pl.BlockSpec(memory_space=pltpu.HBM)] * len(operands),
         out_specs=(
@@ -326,9 +408,10 @@
             pltpu.VMEM(new_kv.shape, jnp.bfloat16),
             pltpu.VMEM(prefill_cache.shape, jnp.bfloat16),
             pltpu.VMEM((n_ctx, 2, slots, block, width), jnp.bfloat16),
+            pltpu.VMEM((2, slots, block, width), jnp.bfloat16),
             pltpu.VMEM((slots, rows, HD), jnp.float32),
             pltpu.VMEM((slots, n_tp * rows, HD), jnp.bfloat16),
-            pltpu.VMEM((2, slots, n_tp * rows, HD), jnp.float32),
+            pltpu.VMEM((slots + 1, n_tp * rows, HD), jnp.float32),
             pltpu.VMEM((2, slots, n_tp * rows, HD), jnp.float32),
             pltpu.SemaphoreType.DMA((4 + 2 * (requests // 8),)),
             pltpu.SemaphoreType.DMA((n_ctx,)),
@@ -337,6 +420,7 @@
             pltpu.SemaphoreType.DMA((n_tp,)),
             pltpu.SemaphoreType.DMA((n_tp,)),
             pltpu.SemaphoreType.DMA((n_tp,)),
+            pltpu.SemaphoreType.DMA((2,)),
             pltpu.SemaphoreType.REGULAR((n_ctx,)),
         ],
         compiler_params=pltpu.CompilerParams(

time: 63.8 us -> 62.5 us (0.980)
  the two profiles are of different devices: /device:TPU:137 before, /device:TPU:249 now
where the time goes in v4:
time: 62.5 us; the launch traced here: 62.4 us
  Pallas kernels  61.7 us (99%)
  between operations  0.64 us (1%)
    pallas_call x1, Pallas kernels, shards(): pl.pallas_call(kernel, out_shape=(jax.ShapeDtypeStruct((2, slots, n_ctx *...  60.4 us
    pallas_call x1, Pallas kernels, shards(): pl.pallas_call(finish, out_shape=(jax.ShapeDtypeStruct(queries.shape, jnp...  1.37 us

profile of v4, /device:TPU:249, one launch (start us, length us, event | category | flops | bytes accessed | tf_op | source)
XLA Modules:
  0.0 62.4 jit_solution(4390300460169696764)
XLA Ops:
  0.6 60.4 %handover.1 = (bf16[2,2,2048,128]{3,2,1,0:T(8,128)(2,1)S(1)}, f32[5,3,16,128]{3,2,1,0:T(8,128)S(1)}) custom-call(bf16[2,32,128,128]{3,2,1,0:T(8,128)(2,1)} %cache_in.1, s32[32]{0:T(128)} %slot_in.1, s32[32]{0:T(128)} %len_in.1, bf16[4,2,512]{2,1,0:T(2,128)(2,1)} %query_in.1, bf16[2,4,2,128]{3,2,1,0:T(2,128)(2,1)} %new_in.1), custom_call_target="tpu_custom_call" | custom-call | tf_op jit(solution)/shard_map/handover/pallas_call | solution.py:393
  61.0 1.4 %finish.1 = (bf16[4,2,512]{2,1,0:T(2,128)(2,1)}, bf16[2,2,2048,128]{3,2,1,0:T(8,128)(2,1)}) custom-call(bf16[2,2,2048,128]{3,2,1,0:T(8,128)(2,1)S(1)} %get-tuple-element.4.rec_ref, f32[5,3,16,128]{3,2,1,0:T(8,128)S(1)} %get-tuple-element.5.box), custom_call_target="tpu_custom_call" | custom-call | tf_op jit(solution)/shard_map/finish/pallas_call | solution.py:431

commit v5 on v4

--- a/solution.py
+++ b/solution.py
@@ -48,7 +48,7 @@
 def kernel(
     cache_in, slot_in, len_in, query_in, new_in,
     rec_ref, box,
-    slot_ref, len_ref, query_ref, new_ref, raw, stage, passing, own_q, all_q, mail, running,
+    slot_ref, len_ref, query_ref, new_ref, raw_keys, raw_values, stage, passing, own_q, all_q, mail, running,
     load_sem, send_sem, recv_sem, q_send_sem, q_recv_sem, mail_send_sem, mail_recv_sem, pass_sem, ready,
 ):
     me = lax.axis_index("ctx")
@@ -59,7 +59,8 @@
     chips = n_ctx // 2
     requests = slot_ref.shape[0]
     slots = requests // n_ctx
-    block = raw.shape[2]
+    block = raw_keys.shape[1]
+    raw = (raw_keys, raw_values)
     own_heads = query_ref.shape[2] // HD
     rows = STEPS * own_heads
 
@@ -67,7 +68,7 @@
         pltpu.make_async_copy(source, target, load_sem.at[i])
         for i, (source, target) in enumerate(
             [(slot_in, slot_ref)]
-            + [(cache_in.at[k, pl.ds(i * 8, 8)], raw.at[k, pl.ds(i * 8, 8)]) for k in range(2) for i in range(requests // 8)]
+            + [(cache_in.at[k, pl.ds(i * 8, 8)], raw[k].at[pl.ds(i * 8, 8)]) for k in range(2) for i in range(requests // 8)]
             + [(query_in, query_ref), (len_in, len_ref), (new_in, new_ref)]
         )
     ]
@@ -98,15 +99,25 @@
             found = jnp.where(slot_ref[r] == slot, r, found)
         return found
 
-    def fill(d, found):
+    def fill(d, found, kinds=range(2)):
         for j in range(slots):
-            for k in range(2):
-                stage[d, k, j] = raw[k, found[j]]
+            for k in kinds:
+                stage[d, k, j] = raw[k][found[j]]
 
     def to(d):
         return pltpu.make_async_remote_copy(
             src_ref=stage.at[d],
             dst_ref=rec_ref.at[:, :, pl.ds(me * block, block)],
+            send_sem=send_sem.at[d],
+            recv_sem=recv_sem.at[me],
+            device_id={"ctx": d},
+            device_id_type=MESH,
+        )
+
+    def part_to(d, k):
+        return pltpu.make_async_remote_copy(
+            src_ref=stage.at[d, k],
+            dst_ref=rec_ref.at[k, :, pl.ds(me * block, block)],
             send_sem=send_sem.at[d],
             recv_sem=recv_sem.at[me],
             device_id={"ctx": d},
@@ -175,10 +186,20 @@
             def _():
                 pl.semaphore_wait(ready.at[d], 1)
 
-            fill(d, now[other * slots : (other + 1) * slots])
+            found = now[other * slots : (other + 1) * slots]
             if other == 0:
-                to(d).start()
+                fill(d, found, [0])
+                part_to(d, 0).start()
+
+                @pl.when(i == 0)
+                def _():
+                    for load in value_loads:
+                        load.wait()
+
+                fill(d, found, [1])
+                part_to(d, 1).start()
             else:
+                fill(d, found)
                 around = (z == HOLDER) & (chip == GOAL)
 
                 @pl.when(around)
@@ -203,7 +224,9 @@
     twin = z * 2 + 1 - core
     loads[0].wait()
     first = requests_of(send_code)
-    for load in loads[1:-3]:
+    parts = (len(loads) - 4) // 2
+    key_loads, value_loads = loads[1 : 1 + parts], loads[1 + parts : -3]
+    for load in key_loads:
         load.wait()
     lax.fori_loop(0, chips - 1, serve, (send_code, first))
     fill(twin, [request_of(twin * slots + j) for j in range(slots)])
@@ -224,7 +247,7 @@
     own = [request_of(me * slots + j) for j in range(slots)]
     for j in range(slots):
         for k in range(2):
-            rec_ref[k, j, pl.ds(me * block, block), :] = raw[k, own[j]]
+            rec_ref[k, j, pl.ds(me * block, block), :] = raw[k][own[j]]
 
     def packed(tops, totals):
         bands = [both[j] for j in range(slots) for both in (tops, totals)]
@@ -319,7 +342,7 @@
     lax.fori_loop(0, chips - 1, collect, recv_code)
 
     mail[slots] = packed([running[0, j] for j in range(slots)], [running[1, j] for j in range(slots)])
-    for k in range(1, n_tp):
+    for k in sorted(range(1, n_tp), key=lambda k: -min(k, n_tp - k)):
         mail_copy(tp, lax.rem(tp + k, n_tp)).start()
     box[tp] = mail[:, pl.ds(tp * rows, rows), :]
 
@@ -406,7 +429,8 @@
             pltpu.SMEM(lengths.shape, jnp.int32),
             pltpu.VMEM(queries.shape, jnp.bfloat16),
             pltpu.VMEM(new_kv.shape, jnp.bfloat16),
-            pltpu.VMEM(prefill_cache.shape, jnp.bfloat16),
+            pltpu.VMEM(prefill_cache.shape[1:], jnp.bfloat16),
+            pltpu.VMEM(prefill_cache.shape[1:], jnp.bfloat16),
             pltpu.VMEM((n_ctx, 2, slots, block, width), jnp.bfloat16),
             pltpu.VMEM((2, slots, block, width), jnp.bfloat16),
             pltpu.VMEM((slots, rows, HD), jnp.float32),

time: 62.5 us -> 61.5 us (0.984)
  Pallas kernels: 61.7 us -> 60.7 us
    pallas_call x1, Pallas kernels: 60.4 us -> 59.4 us  [shards(): pl.pallas_call(kernel, out_shape=(jax.ShapeDtypeStruct((2, slots, n_ctx *...]
where the time goes in v5:
time: 61.5 us; the launch traced here: 61.4 us
  Pallas kernels  60.7 us (99%)
  between operations  0.64 us (1%)
    pallas_call x1, Pallas kernels, shards(): pl.pallas_call(kernel, out_shape=(jax.ShapeDtypeStruct((2, slots, n_ctx *...  59.4 us
    pallas_call x1, Pallas kernels, shards(): pl.pallas_call(finish, out_shape=(jax.ShapeDtypeStruct(queries.shape, jnp...  1.37 us

profile of v5, /device:TPU:249, one launch (start us, length us, event | category | flops | bytes accessed | tf_op | source)
XLA Modules:
  0.0 61.4 jit_solution(9156231544232539406)
XLA Ops:
  0.6 59.4 %handover.1 = (bf16[2,2,2048,128]{3,2,1,0:T(8,128)(2,1)S(1)}, f32[5,3,16,128]{3,2,1,0:T(8,128)S(1)}) custom-call(bf16[2,32,128,128]{3,2,1,0:T(8,128)(2,1)} %cache_in.1, s32[32]{0:T(128)} %slot_in.1, s32[32]{0:T(128)} %len_in.1, bf16[4,2,512]{2,1,0:T(2,128)(2,1)} %query_in.1, bf16[2,4,2,128]{3,2,1,0:T(2,128)(2,1)} %new_in.1), custom_call_target="tpu_custom_call" | custom-call | tf_op jit(solution)/shard_map/handover/pallas_call | solution.py:416
  60.0 1.4 %finish.1 = (bf16[4,2,512]{2,1,0:T(2,128)(2,1)}, bf16[2,2,2048,128]{3,2,1,0:T(8,128)(2,1)}) custom-call(bf16[2,2,2048,128]{3,2,1,0:T(8,128)(2,1)S(1)} %get-tuple-element.4.rec_ref, f32[5,3,16,128]{3,2,1,0:T(8,128)S(1)} %get-tuple-element.5.box), custom_call_target="tpu_custom_call" | custom-call | tf_op jit(solution)/shard_map/finish/pallas_call | solution.py:455

commit v6 on v5

--- a/solution.py
+++ b/solution.py
@@ -124,24 +124,36 @@
             device_id_type=MESH,
         )
 
-    def to_via(d):
-        return pltpu.make_async_remote_copy(
-            src_ref=stage.at[d],
-            dst_ref=passing,
+    round_parts = ((0, slots), (1, slots - 1))
+
+    def to_via(d, k, count):
+        return pltpu.make_async_remote_copy(
+            src_ref=stage.at[d, k, pl.ds(0, count)],
+            dst_ref=passing.at[k, pl.ds(0, count)],
             send_sem=send_sem.at[d],
-            recv_sem=pass_sem.at[0],
+            recv_sem=pass_sem.at[0, k],
             device_id={"ctx": VIA * 2 + core},
             device_id_type=MESH,
         )
 
-    def pass_on():
+    def pass_on(k, count):
         source = HOLDER * 2 + core
         return pltpu.make_async_remote_copy(
-            src_ref=passing,
-            dst_ref=rec_ref.at[:, :, pl.ds(source * block, block)],
-            send_sem=pass_sem.at[1],
+            src_ref=passing.at[k, pl.ds(0, count)],
+            dst_ref=rec_ref.at[k, pl.ds(0, count), pl.ds(source * block, block)],
+            send_sem=pass_sem.at[1, k],
             recv_sem=recv_sem.at[source],
             device_id={"ctx": GOAL * 2 + 1 - core},
+            device_id_type=MESH,
+        )
+
+    def last_values_to(d):
+        return pltpu.make_async_remote_copy(
+            src_ref=stage.at[d, 1, pl.ds(slots - 1, 1)],
+            dst_ref=rec_ref.at[1, pl.ds(slots - 1, 1), pl.ds(me * block, block)],
+            send_sem=send_sem.at[d],
+            recv_sem=recv_sem.at[me],
+            device_id={"ctx": d},
             device_id_type=MESH,
         )
 
@@ -175,8 +187,9 @@
 
         @pl.when((z == VIA) & (i == TURN))
         def _():
-            to_via(GOAL * 2 + 1 - core).wait_recv()
-            pass_on().start()
+            for k, count in round_parts:
+                to_via(GOAL * 2 + 1 - core, k, count).wait_recv()
+                pass_on(k, count).start()
 
         chip = lax.rem(z + lax.rem(code, chips), chips)
         for other in range(2):
@@ -204,7 +217,9 @@
 
                 @pl.when(around)
                 def _():
-                    to_via(d).start()
+                    for k, count in round_parts:
+                        to_via(d, k, count).start()
+                    last_values_to(d).start()
 
                 @pl.when(jnp.logical_not(around))
                 def _():
@@ -354,7 +369,8 @@
 
     @pl.when(z == VIA)
     def _():
-        pass_on().wait_send()
+        for k, count in round_parts:
+            pass_on(k, count).wait_send()
 
     for k in range(1, n_tp):
         q_copy(tp, lax.rem(tp + k, n_tp)).wait_send()
@@ -444,7 +460,7 @@
             pltpu.SemaphoreType.DMA((n_tp,)),
             pltpu.SemaphoreType.DMA((n_tp,)),
             pltpu.SemaphoreType.DMA((n_tp,)),
-            pltpu.SemaphoreType.DMA((2,)),
+            pltpu.SemaphoreType.DMA((2, 2)),
             pltpu.SemaphoreType.REGULAR((n_ctx,)),
         ],
         compiler_params=pltpu.CompilerParams(

time: 61.5 us -> 61.2 us (level)
  the two profiles are of different devices: /device:TPU:249 before, /device:TPU:201 now
where the time goes in v6:
time: 61.2 us; the launch traced here: 61.1 us
  Pallas kernels  60.4 us (99%)
  between operations  0.64 us (1%)
    pallas_call x1, Pallas kernels, shards(): pl.pallas_call(kernel, out_shape=(jax.ShapeDtypeStruct((2, slots, n_ctx *...  59.1 us
    pallas_call x1, Pallas kernels, shards(): pl.pallas_call(finish, out_shape=(jax.ShapeDtypeStruct(queries.shape, jnp...  1.37 us

profile of v6, /device:TPU:201, one launch (start us, length us, event | category | flops | bytes accessed | tf_op | source)
XLA Modules:
  0.0 61.1 jit_solution(7373410707074566560)
XLA Ops:
  0.6 59.1 %handover.1 = (bf16[2,2,2048,128]{3,2,1,0:T(8,128)(2,1)S(1)}, f32[5,3,16,128]{3,2,1,0:T(8,128)S(1)}) custom-call(bf16[2,32,128,128]{3,2,1,0:T(8,128)(2,1)} %cache_in.1, s32[32]{0:T(128)} %slot_in.1, s32[32]{0:T(128)} %len_in.1, bf16[4,2,512]{2,1,0:T(2,128)(2,1)} %query_in.1, bf16[2,4,2,128]{3,2,1,0:T(2,128)(2,1)} %new_in.1), custom_call_target="tpu_custom_call" | custom-call | tf_op jit(solution)/shard_map/handover/pallas_call | solution.py:432
  59.7 1.4 %finish.1 = (bf16[4,2,512]{2,1,0:T(2,128)(2,1)}, bf16[2,2,2048,128]{3,2,1,0:T(8,128)(2,1)}) custom-call(bf16[2,2,2048,128]{3,2,1,0:T(8,128)(2,1)S(1)} %get-tuple-element.4.rec_ref, f32[5,3,16,128]{3,2,1,0:T(8,128)S(1)} %get-tuple-element.5.box), custom_call_target="tpu_custom_call" | custom-call | tf_op jit(solution)/shard_map/finish/pallas_call | solution.py:471

commit v7 on v6

--- a/solution.py
+++ b/solution.py
@@ -15,25 +15,25 @@
 FLOOR = -1e30
 
 SEND_ORDER = (
-    (3, 5, 2, 7, 1, 4, 6),
-    (2, 1, 4, 7, 6, 5, 3),
-    (1, 3, 7, 6, 2, 4, 5),
-    (5, 1, 2, 3, 6, 7, 4),
-    (5, 4, 2, 6, 7, 1, 3),
-    (3, 4, 7, 1, 5, 2, 6),
-    (6, 2, 5, 3, 1, 4, 7),
-    (1, 5, 4, 2, 6, 7, 3),
+    (3, 5, 2, 4, 6, 1, 7),
+    (7, 3, 6, 5, 4, 1, 2),
+    (1, 7, 4, 2, 6, 3, 5),
+    (6, 1, 2, 5, 7, 4, 3),
+    (6, 4, 2, 5, 3, 7, 1),
+    (3, 4, 5, 7, 1, 6, 2),
+    (6, 5, 3, 1, 7, 2, 4),
+    (2, 6, 1, 5, 4, 3, 7),
 )
 HOLDER, VIA, GOAL, TURN = 4, 3, 0, 4
 RECV_ORDER = (
-    (1, 5, 3, 6, 4, 7, 2),
-    (4, 3, 7, 1, 5, 2, 6),
-    (6, 2, 7, 1, 5, 3, 4),
-    (5, 7, 6, 4, 3, 2, 1),
-    (7, 1, 3, 4, 2, 5, 6),
-    (4, 6, 3, 5, 7, 2, 1),
-    (6, 7, 3, 2, 4, 1, 5),
-    (2, 1, 6, 5, 7, 3, 4),
+    (1, 2, 7, 5, 3, 6, 4),
+    (4, 1, 5, 2, 6, 7, 3),
+    (2, 6, 3, 7, 1, 5, 4),
+    (5, 7, 3, 6, 4, 2, 1),
+    (7, 2, 5, 4, 1, 3, 6),
+    (2, 3, 7, 6, 4, 5, 1),
+    (6, 3, 4, 2, 7, 1, 5),
+    (2, 7, 5, 1, 3, 6, 4),
 )
 
 

time: 61.2 us -> 61.3 us (level)
  the two profiles are of different devices: /device:TPU:201 before, /device:TPU:225 now
where the time goes in v7:
time: 61.3 us; the launch traced here: 61.2 us
  Pallas kernels  60.5 us (99%)
  between operations  0.64 us (1%)
    pallas_call x1, Pallas kernels, shards(): pl.pallas_call(kernel, out_shape=(jax.ShapeDtypeStruct((2, slots, n_ctx *...  59.2 us
    pallas_call x1, Pallas kernels, shards(): pl.pallas_call(finish, out_shape=(jax.ShapeDtypeStruct(queries.shape, jnp...  1.37 us

profile of v7, /device:TPU:225, one launch (start us, length us, event | category | flops | bytes accessed | tf_op | source)
XLA Modules:
  0.0 61.2 jit_solution(14228024109281730005)
XLA Ops:
  0.6 59.2 %handover.1 = (bf16[2,2,2048,128]{3,2,1,0:T(8,128)(2,1)S(1)}, f32[5,3,16,128]{3,2,1,0:T(8,128)S(1)}) custom-call(bf16[2,32,128,128]{3,2,1,0:T(8,128)(2,1)} %cache_in.1, s32[32]{0:T(128)} %slot_in.1, s32[32]{0:T(128)} %len_in.1, bf16[4,2,512]{2,1,0:T(2,128)(2,1)} %query_in.1, bf16[2,4,2,128]{3,2,1,0:T(2,128)(2,1)} %new_in.1), custom_call_target="tpu_custom_call" | custom-call | tf_op jit(solution)/shard_map/handover/pallas_call | solution.py:432
  59.8 1.4 %finish.1 = (bf16[4,2,512]{2,1,0:T(2,128)(2,1)}, bf16[2,2,2048,128]{3,2,1,0:T(8,128)(2,1)}) custom-call(bf16[2,2,2048,128]{3,2,1,0:T(8,128)(2,1)S(1)} %get-tuple-element.4.rec_ref, f32[5,3,16,128]{3,2,1,0:T(8,128)S(1)} %get-tuple-element.5.box), custom_call_target="tpu_custom_call" | custom-call | tf_op jit(solution)/shard_map/finish/pallas_call | solution.py:471
